TPU v7x, 32 devices: a whole 2x2x4 slice. The times are simulated.
32 devices in a mesh: groups: 2 (over x), blk: 16 (over z, y, core).
Axes of the slice: x: 2, y: 2, z: 4, core: 2. Of those that a mesh axis runs over, the one named last changes fastest.
Arguments:
- hidden: bfloat16 [12288, 5120], P(('groups', 'blk')), parts along dimension 0, may hold values from -6 to 6
- norm_gain: float32 [5120], replicated, may hold values from 0.5 to 1.5
- q_weight: bfloat16 [5120, 2560], P('blk'), may hold values from -0.078125 to 0.078125
- q_bias: float32 [2560], replicated, may hold values from -5 to 5
- kv_store: bfloat16 [128, 2, 512, 512], P(('groups', 'blk')), parts along dimension 0, may hold values from -620 to 620
- block_home: int32 [128], P('groups'), parts along dimension 0, may hold values from 0 to 63, as said below
- need_ids: int32 [64, 2], P(('groups', 'blk')), parts along dimension 0, may hold values from 0 to 63, as said below
- hole_pos: int32 [64], P(('groups', 'blk')), parts along dimension 0, may hold values from 0 to 32767, as said below
- fill_len: int32 [64], P(('groups', 'blk')), parts along dimension 0, may hold values from 48 to 192
Outputs:
- attended: bfloat16 [12288, 2560], P(('groups', 'blk')), parts along dimension 0
There are 2 independent parts, one for each index of `groups`. A program takes and returns all parts, laid end to end along the dimension named above; an argument that names none is the same for every part. Nothing has to cross between parts.
Inputs may be any that keep to these rules, and one draw needn't show every extreme that they name: block_home is a permutation; block b is kept by device block_home[b] // 4 of blk. `need_ids`: the 4 blocks listed by the candidates of one device of blk are all different and are kept by different devices, each at most 2 places away from it along blk, counted around the loop. The span from hole_pos to hole_pos + fill_len - 1 lies inside the first block that the candidate lists.
All inputs are finite; a program needn't handle non-finite values.
Results may differ from a plain program's by a relative error of at most 0.0035.
The roundings to bfloat16 on the way count: a program that leaves them out, or rounds other values in their place, can miss the bound.
Values may be sent and summed in bfloat16 or wider, within the bound.
A program may use at most 128 MiB of HBM per device.

v0:
```python
import math
import jax
import jax.numpy as jnp
from jax import lax
from jax.sharding import PartitionSpec as P

HEAD_SIZE = 128
QUERY_HEADS = 20
KEY_HEADS = 4
BLOCK_TOKENS = 512
BLOCKS_NEEDED = 2
REACH = 2


def passed_along(block, axis, distance):
    devices = range(lax.axis_size(axis))
    route = [((i - distance) % len(devices), i) for i in devices]
    return lax.ppermute(block, axis, route)


def rms_normed(hidden, norm_gain):
    widened = hidden.astype(jnp.float32)
    scale_inv = lax.rsqrt(jnp.mean(widened * widened, axis=-1, keepdims=True) + 1e-06)
    return (widened * scale_inv * norm_gain).astype(jnp.bfloat16)


def attend_single(packed):
    candidate_query_rows, sketch_blocks, block_ids, hole_start, fill_rows = packed
    count_of_rows = candidate_query_rows.shape[0]
    block_key_rows = sketch_blocks[:, 0].reshape(BLOCKS_NEEDED * BLOCK_TOKENS, KEY_HEADS, HEAD_SIZE)
    block_value_rows = sketch_blocks[:, 1].reshape(
        BLOCKS_NEEDED * BLOCK_TOKENS, KEY_HEADS, HEAD_SIZE
    )
    query_matrix = candidate_query_rows.reshape(
        count_of_rows, KEY_HEADS, QUERY_HEADS // KEY_HEADS, HEAD_SIZE
    )
    scores = jnp.einsum(
        "rkgd,tkd->rkgt", query_matrix, block_key_rows, preferred_element_type=jnp.float32
    ) / math.sqrt(HEAD_SIZE)
    position = (
        block_ids[:, None] * BLOCK_TOKENS + jnp.arange(BLOCK_TOKENS, dtype=jnp.int32)[None, :]
    ).reshape(BLOCKS_NEEDED * BLOCK_TOKENS)
    masked = (position >= hole_start) & (position < hole_start + fill_rows)
    scores = jnp.where(masked[None, None, None, :], jnp.float32(-1e30), scores)
    row_max = jnp.max(scores, axis=-1, keepdims=True)
    exponent = jnp.exp(scores - row_max)
    denominator = jnp.sum(exponent, axis=-1)
    weights = exponent.astype(jnp.bfloat16)
    attended = (
        jnp.einsum("rkgt,tkd->rkgd", weights, block_value_rows, preferred_element_type=jnp.float32)
        / denominator[..., None]
    )
    attended = attended.reshape(count_of_rows, QUERY_HEADS * HEAD_SIZE)
    live_rows = jnp.arange(count_of_rows, dtype=jnp.int32) < fill_rows
    return jnp.where(live_rows[:, None], attended, jnp.float32(0.0)).astype(jnp.bfloat16)


def attend_all(query, sketch_blocks, block_lists, hole_starts, fill_rows):
    cand_count = block_lists.shape[0]
    count_of_rows = query.shape[0] // cand_count
    shaped = query.reshape(cand_count, count_of_rows, QUERY_HEADS * HEAD_SIZE)
    results = lax.map(attend_single, (shaped, sketch_blocks, block_lists, hole_starts, fill_rows))
    return results.reshape(cand_count * count_of_rows, QUERY_HEADS * HEAD_SIZE)


def shards(hidden, norm_gain, q_weight, q_bias, kv_store, block_home, need_ids, hole_pos, fill_len):
    normed = rms_normed(hidden, norm_gain)
    whole_weight = lax.all_gather(q_weight, "blk", axis=0, tiled=True)
    projected = jnp.dot(normed, whole_weight, preferred_element_type=jnp.float32)
    query = (projected + q_bias).astype(jnp.bfloat16)
    device_count = lax.axis_size("blk")
    myself = lax.axis_index("blk")
    local_count = kv_store.shape[0]
    empty_block = jnp.zeros(kv_store.shape[1:], kv_store.dtype)

    def select_block(block_lists):
        stored_at = block_home[block_lists.reshape(-1)]
        owned_here = stored_at // local_count == myself
        slot_index = jnp.sum(jnp.where(owned_here, stored_at % local_count, 0))
        has_block = jnp.any(owned_here)
        chosen = lax.dynamic_index_in_dim(kv_store, slot_index, 0, keepdims=False)
        return jnp.where(has_block, chosen, empty_block)

    incoming = []
    for offset in range(-REACH, REACH + 1):
        if offset == 0:
            incoming.append(select_block(need_ids))
        else:
            asked = passed_along(need_ids, "blk", -offset)
            incoming.append(passed_along(select_block(asked), "blk", offset))
    arrived = jnp.stack(incoming, axis=0)
    owners = block_home[need_ids] // local_count
    slot_of_entry = jnp.remainder(myself - owners + REACH, device_count)
    sketch_blocks = jnp.take(arrived, slot_of_entry, axis=0)
    return attend_all(query, sketch_blocks, need_ids, hole_pos, fill_len)


def solution(mesh):
    placed = (
        P(("groups", "blk"), None),
        P(),
        P("blk", None),
        P(),
        P(("groups", "blk"), None, None, None),
        P("groups"),
        P(("groups", "blk"), None),
        P(("groups", "blk")),
        P(("groups", "blk")),
    )
    return jax.shard_map(
        shards, mesh=mesh, in_specs=placed, out_specs=P(("groups", "blk"), None), check_vma=False
    )
```

profile of v0, /device:TPU:0, one launch (start us, length us, event | category | flops | bytes accessed | tf_op | source)
XLA Modules:
  0.0 285.8 jit_solution(10790405811085733742)
XLA Ops:
  7.8 2.6 collective-permute-start
  10.3 4.1 %collective-permute-start.4 = (s32[2,2]{1,0:T(2,128)}, s32[2,2]{1,0:T(2,128)S(1)}, u32[]{:S(2)}, u32[]{:S(2)}) collective-permute-start(s32[2,2]{1,0:T(2,128)} %param.17), channel_id=1, source_target_pairs={{1,0},{2,1},{3,2},{4,3},{5,4},{6,5},{7,6},{8,7},{9,8},{10,9},{11,1... | collective-permute-start | bytes 56 | tf_op jit(solution)/shard_map/ppermute | solution.py:18
  29.1 4.0 %select_bitcast_fusion.2 = (bf16[2,512,512]{2,1,0:T(8,128)(2,1)S(1)}, bf16[2,512,512]{2,1,0:T(8,128)(2,1)}) fusion(bf16[4,2,512,512]{3,2,1,0:T(8,128)(2,1)} %param.15, s32[]{:T(128)S(6)} %select_n.257, pred[]{:T(512)} %get-tuple-element.77, s32[]{:T(128)S(6)} %select_n.249, pred[]{:T(512)} %get-tuple-element.92), kind=kLoop, calls=%fused_computation.48 | loop fusion | flops 1048576 | bytes 4194314 | tf_op jit(solution)/shard_map/jit(_where)/select_n | solution.py:82
  33.1 2.8 collective-permute-start.1
  43.1 38.2 %collective-permute-done.1 = bf16[2,512,512]{2,1,0:T(8,128)(2,1)S(1)} collective-permute-done((bf16[2,512,512]{2,1,0:T(8,128)(2,1)}, bf16[2,512,512]{2,1,0:T(8,128)(2,1)S(1)}, u32[]{:S(2)}, u32[]{:S(2)}) %collective-permute-start.1) | collective-permute-done | bytes 1048608 | tf_op jit(solution)/shard_map/ppermute | solution.py:18
  81.3 33.3 %collective-permute-done.3 = bf16[2,512,512]{2,1,0:T(8,128)(2,1)S(1)} collective-permute-done((bf16[2,512,512]{2,1,0:T(8,128)(2,1)S(1)}, bf16[2,512,512]{2,1,0:T(8,128)(2,1)S(1)}, u32[]{:S(2)}, u32[]{:S(2)}) %collective-permute-start.3) | collective-permute-done | bytes 1048608 | tf_op jit(solution)/shard_map/ppermute | solution.py:18
  114.7 2.4 select_bitcast_fusion
  117.1 2.4 copy-done.4
  120.1 1.2 collective-permute-start.7
  121.4 3.0 %fusion.15 = f32[384]{0:T(512)S(1)} fusion(bf16[384,5120]{1,0:T(8,128)(2,1)} %param.11), kind=kLoop, calls=%fused_computation.33 | loop fusion | flops 5897856 | bytes 3933696 | tf_op jit(solution)/shard_map/reduce_sum | solution.py:23
  124.5 45.0 %collective-permute-done.5 = bf16[2,512,512]{2,1,0:T(8,128)(2,1)S(1)} collective-permute-done((bf16[2,512,512]{2,1,0:T(8,128)(2,1)S(1)}, bf16[2,512,512]{2,1,0:T(8,128)(2,1)S(1)}, u32[]{:S(2)}, u32[]{:S(2)}) %collective-permute-start.5) | collective-permute-done | bytes 1048608 | tf_op jit(solution)/shard_map/ppermute | solution.py:18
  172.3 5.3 %gather_fusion.6 = bf16[4,2,512,512]{3,2,1,0:T(8,128)(2,1)} fusion(bf16[5,2,512,512]{3,2,1,0:T(8,128)(2,1)} %bitcast_dynamic-update-slice_fusion, s32[1024]{0:T(1024)S(1)} %pad_clamp_fusion), kind=kCustom, calls=%fused_computation.6 | custom fusion | bytes 8388624 | tf_op jit(solution)/shard_map/jit(_take)/gather | solution.py:94
  177.6 4.7 %broadcast_select_fusion = bf16[2,2,2,512,512]{4,3,2,1,0:T(8,128)(2,1)} fusion(bf16[2,2,2,512,512]{4,3,2,1,0:T(8,128)(2,1)} %bitcast.95, pred[2,2]{1,0:T(4,128)(4,1)S(1)} %compare_and_fusion.1), kind=kLoop, calls=%fused_computation.38 | loop fusion | flops 2097152 | bytes 8388612 | tf_op jit(solution)/shard_map/jit(_take)/select_n | solution.py:94
  182.3 30.0 %all-gather.2.cloned.1.call-done = bf16[5120,2560]{1,0:T(8,128)(2,1)} async-done(((bf16[320,2560]{1,0:T(8,128)(2,1)}), bf16[5120,2560]{1,0:T(8,128)(2,1)}) %all-gather.2.cloned.1.call-update) | async-done | bytes 26214416 | tf_op jit(solution)/shard_map/all_gather | solution.py:68
  212.3 17.5 %fusion.18 = bf16[384,2560]{1,0:T(8,128)(2,1)} fusion(bf16[5120,2560]{1,0:T(8,128)(2,1)} %all-gather.2.cloned.1.call-done, bf16[384,5120]{1,0:T(8,128)(2,1)} %param.11, f32[5120]{0:T(1024)S(1)} %copy-done.6, f32[384]{0:T(512)S(1)} %add_rsqrt_fusion, f32[2560]{0:T(1024)S(1)} %copy-done.7), kind=kOutput, calls=%fused_computation.37 | convolution fusion | flops 10076160000 | bytes 32144896 | tf_op jit(solution)/shard_map/dot_general | solution.py:69
  229.8 48.5 %while.10 = (s32[]{:T(128)}, bf16[2,192,2560]{2,1,0:T(8,128)(2,1)}, s32[2]{0:T(128)S(1)}, bf16[2,2,2,512,512]{4,3,2,1,0:T(8,128)(2,1)}, s32[2,2]{1,0:T(2,128)S(1...) while((s32[]{:T(128)}, bf16[2,192,2560]{2,1,0:T(8,128)(2,1)}, s32[2]{0:T(128)S(1)}, ...), condition=%wide.region_14.15_spmd, body=%wide.region_11.14_spmd.sunk | while | flops 2057990912 | bytes 79906376 | solution.py:62
  233.5 1.3 constant_dynamic-slice_fusion.7
  235.3 1.7 copy_bitcast_fusion.2
  237.1 1.2 fusion.47
  238.3 1.3 squeeze.29
  239.6 1.1 squeeze.30
  240.8 2.9 %bitcast_reduce_fusion.2 = (f32[192,4,5]{0,2,1:T(8,128)S(1)}, f32[4,1024,192,5]{1,2,3,0:T(8,128)S(1)}) fusion(pred[1024]{0:T(1024)(128)(4,1)S(1)} %and.179, bf16[192,4,5,128]{0,3,2,1:T(8,128)(2,1)S(1)} %bitcast.91, bf16[1024,4,128,1]{2,1,0,3:T(4,128)(2,1)S(1)} %bitcast.93), kind=kOutput, calls=%fused_computation.8.clone.1 | convolution fusion | flops 1018425600 | bytes 17776640 | tf_op jit(solution)/shard_map/while/body/eval_jaxpr/rkgd,tkd->rkgt/dot_general | solution.py:37
  243.7 3.9 %fusion.48 = f32[192,4,5]{0,2,1:T(8,128)S(1)} fusion(f32[4,1024,192,5]{1,2,3,0:T(8,128)S(1)} %get-tuple-element.144, f32[192,4,5]{0,2,1:T(8,128)S(1)} %get-tuple-element.145, pred[1024]{0:T(1024)(128)(4,1)S(1)} %and.179), kind=kLoop, calls=%fused_computation.11.clone.1 | loop fusion | flops 15724800 | bytes 15760384 | tf_op jit(solution)/shard_map/while/body/eval_jaxpr/reduce_sum | solution.py:47
  247.7 3.9 %bitcast_divide_fusion.2 = bf16[192,4,5,128]{3,0,2,1:T(8,128)(2,1)S(1)} fusion(f32[4,1024,192,5]{1,2,3,0:T(8,128)S(1)} %get-tuple-element.144, f32[192,4,5]{0,2,1:T(8,128)S(1)} %get-tuple-element.145, pred[1024]{0:T(1024)(128)(4,1)S(1)} %and.179, bf16[1024,4,128,1]{2,1,0,3:T(4,128)(2,1)S(1)} %bitcast.94, f32[192,4,5]{0,2,1:T(8,128)S(1)} %fusion.48), kind=kOutput, calls=%fused_computation.17.clone.1 | convolution fusion | flops 1023344640 | bytes 17792000 | tf_op jit(solution)/shard_map/while/body/eval_jaxpr/rkgt,tkd->rkgd/dot_general | solution.py:50
  257.7 1.3 constant_dynamic-slice_fusion.7
  259.6 1.7 copy_bitcast_fusion.2
  261.3 1.2 fusion.47
  262.5 1.3 squeeze.29
  263.8 1.1 squeeze.30
  265.0 2.9 %bitcast_reduce_fusion.2 = (f32[192,4,5]{0,2,1:T(8,128)S(1)}, f32[4,1024,192,5]{1,2,3,0:T(8,128)S(1)}) fusion(pred[1024]{0:T(1024)(128)(4,1)S(1)} %and.179, bf16[192,4,5,128]{0,3,2,1:T(8,128)(2,1)S(1)} %bitcast.91, bf16[1024,4,128,1]{2,1,0,3:T(4,128)(2,1)S(1)} %bitcast.93), kind=kOutput, calls=%fused_computation.8.clone.1 | convolution fusion | flops 1018425600 | bytes 17776640 | tf_op jit(solution)/shard_map/while/body/eval_jaxpr/rkgd,tkd->rkgt/dot_general | solution.py:37
  267.9 3.9 %fusion.48 = f32[192,4,5]{0,2,1:T(8,128)S(1)} fusion(f32[4,1024,192,5]{1,2,3,0:T(8,128)S(1)} %get-tuple-element.144, f32[192,4,5]{0,2,1:T(8,128)S(1)} %get-tuple-element.145, pred[1024]{0:T(1024)(128)(4,1)S(1)} %and.179), kind=kLoop, calls=%fused_computation.11.clone.1 | loop fusion | flops 15724800 | bytes 15760384 | tf_op jit(solution)/shard_map/while/body/eval_jaxpr/reduce_sum | solution.py:47
  271.9 3.9 %bitcast_divide_fusion.2 = bf16[192,4,5,128]{3,0,2,1:T(8,128)(2,1)S(1)} fusion(f32[4,1024,192,5]{1,2,3,0:T(8,128)S(1)} %get-tuple-element.144, f32[192,4,5]{0,2,1:T(8,128)S(1)} %get-tuple-element.145, pred[1024]{0:T(1024)(128)(4,1)S(1)} %and.179, bf16[1024,4,128,1]{2,1,0,3:T(4,128)(2,1)S(1)} %bitcast.94, f32[192,4,5]{0,2,1:T(8,128)S(1)} %fusion.48), kind=kOutput, calls=%fused_computation.17.clone.1 | convolution fusion | flops 1023344640 | bytes 17792000 | tf_op jit(solution)/shard_map/while/body/eval_jaxpr/rkgt,tkd->rkgd/dot_general | solution.py:50
  (97 shorter events, 28.6 us)
Async XLA Ops:
  6.5 10.1 %copy-start = (s32[64]{0:T(128)S(1)}, s32[64]{0:T(128)}, u32[]{:S(2)}) copy-start(s32[64]{0:T(128)} %param.16) | copy-start | bytes 772
  6.5 205.8 %all-gather.2.cloned.1.call-start = ((), (), s32[]{:S(2)}) async-start(), calls=%async_computation | async-start | bytes 27852800 | tf_op jit(solution)/shard_map/all_gather | solution.py:68
  7.3 14.2 %collective-permute-start.2 = (s32[2,2]{1,0:T(2,128)}, s32[2,2]{1,0:T(2,128)S(1)}, u32[]{:S(2)}, u32[]{:S(2)}) collective-permute-start(s32[2,2]{1,0:T(2,128)} %param.17), channel_id=1, source_target_pairs={{15,0},{0,1},{1,2},{2,3},{3,4},{4,5},{5,6},{6,7},{7,8},{8,9},{9,10... | collective-permute-start | bytes 56 | tf_op jit(solution)/shard_map/ppermute | solution.py:18
  7.8 14.5 %collective-permute-start = (s32[2,2]{1,0:T(2,128)}, s32[2,2]{1,0:T(2,128)S(1)}, u32[]{:S(2)}, u32[]{:S(2)}) collective-permute-start(s32[2,2]{1,0:T(2,128)} %param.17), channel_id=1, source_target_pairs={{14,0},{15,1},{0,2},{1,3},{2,4},{3,5},{4,6},{5,7},{6,8},{7,9},{8,1... | collective-permute-start | bytes 56 | tf_op jit(solution)/shard_map/ppermute | solution.py:18
  10.3 25.5 %collective-permute-start.4 = (s32[2,2]{1,0:T(2,128)}, s32[2,2]{1,0:T(2,128)S(1)}, u32[]{:S(2)}, u32[]{:S(2)}) collective-permute-start(s32[2,2]{1,0:T(2,128)} %param.17), channel_id=1, source_target_pairs={{1,0},{2,1},{3,2},{4,3},{5,4},{6,5},{7,6},{8,7},{9,8},{10,9},{11,1... | collective-permute-start | bytes 56 | tf_op jit(solution)/shard_map/ppermute | solution.py:18
  14.4 22.1 %collective-permute-start.6 = (s32[2,2]{1,0:T(2,128)}, s32[2,2]{1,0:T(2,128)S(1)}, u32[]{:S(2)}, u32[]{:S(2)}) collective-permute-start(s32[2,2]{1,0:T(2,128)} %param.17), channel_id=1, source_target_pairs={{2,0},{3,1},{4,2},{5,3},{6,4},{7,5},{8,6},{9,7},{10,8},{11,9},{12,... | collective-permute-start | bytes 56 | tf_op jit(solution)/shard_map/ppermute | solution.py:18
  33.1 48.2 %collective-permute-start.1 = (bf16[2,512,512]{2,1,0:T(8,128)(2,1)}, bf16[2,512,512]{2,1,0:T(8,128)(2,1)S(1)}, u32[]{:S(2)}, u32[]{:S(2)}) collective-permute-start(bf16[2,512,512]{2,1,0:T(8,128)(2,1)} %get-tuple-element.89), channel_id=1, source_target_pairs={{2,0},{3,1},{4,2},{5,3},{6,4},{7,5},{8,6},{9,7},{10,8},{11,9},{12,... | collective-permute-start | bytes 3145736 | tf_op jit(solution)/shard_map/ppermute | solution.py:18
  36.6 78.1 %collective-permute-start.3 = (bf16[2,512,512]{2,1,0:T(8,128)(2,1)S(1)}, bf16[2,512,512]{2,1,0:T(8,128)(2,1)S(1)}, u32[]{:S(2)}, u32[]{:S(2)}) collective-permute-start(bf16[2,512,512]{2,1,0:T(8,128)(2,1)S(1)} %get-tuple-element.88), channel_id=1, source_target_pairs={{1,0},{2,1},{3,2},{4,3},{5,4},{6,5},{7,6},{8,7},{9,8},{10,9},{11,1... | collective-permute-start | bytes 3145736 | tf_op jit(solution)/shard_map/ppermute | solution.py:18
  43.1 71.7 %copy-start.3 = (bf16[4,2,512,512]{3,2,1,0:T(8,128)(2,1)S(1)}, bf16[4,2,512,512]{3,2,1,0:T(8,128)(2,1)}, u32[]{:S(2)}) copy-start(bf16[4,2,512,512]{3,2,1,0:T(8,128)(2,1)} %param.15) | copy-start | bytes 12582916
  117.1 2.4 copy-start.4
  119.5 49.9 %collective-permute-start.5 = (bf16[2,512,512]{2,1,0:T(8,128)(2,1)S(1)}, bf16[2,512,512]{2,1,0:T(8,128)(2,1)S(1)}, u32[]{:S(2)}, u32[]{:S(2)}) collective-permute-start(bf16[2,512,512]{2,1,0:T(8,128)(2,1)S(1)} %get-tuple-element.87), channel_id=1, source_target_pairs={{15,0},{0,1},{1,2},{2,3},{3,4},{4,5},{5,6},{6,7},{7,8},{8,9},{9,10... | collective-permute-start | bytes 3145736 | tf_op jit(solution)/shard_map/ppermute | solution.py:18
  120.1 51.1 %collective-permute-start.7 = (bf16[2,512,512]{2,1,0:T(8,128)(2,1)S(1)}, bf16[2,512,512]{2,1,0:T(8,128)(2,1)S(1)}, u32[]{:S(2)}, u32[]{:S(2)}) collective-permute-start(bf16[2,512,512]{2,1,0:T(8,128)(2,1)S(1)} %get-tuple-element.85), channel_id=1, source_target_pairs={{14,0},{15,1},{0,2},{1,3},{2,4},{3,5},{4,6},{5,7},{6,8},{7,9},{8,1... | collective-permute-start | bytes 3145736 | tf_op jit(solution)/shard_map/ppermute | solution.py:18
  177.6 34.8 %copy-start.6 = (f32[5120]{0:T(1024)S(1)}, f32[5120]{0:T(1024)}, u32[]{:S(2)}) copy-start(f32[5120]{0:T(1024)} %param.12) | copy-start | bytes 61444
  177.6 34.8 %copy-start.7 = (f32[2560]{0:T(1024)S(1)}, f32[2560]{0:T(1024)}, u32[]{:S(2)}) copy-start(f32[2560]{0:T(1024)} %param.14) | copy-start | bytes 30724
  182.3 47.5 %copy-start.5 = (s32[2,2]{1,0:T(2,128)S(1)}, s32[2,2]{1,0:T(2,128)}, u32[]{:S(2)}) copy-start(s32[2,2]{1,0:T(2,128)} %param.17) | copy-start | bytes 52
  182.3 47.5 %copy-start.8 = (s32[2]{0:T(128)S(1)}, s32[2]{0:T(128)}, u32[]{:S(2)}) copy-start(s32[2]{0:T(128)} %param.19) | copy-start | bytes 28
  182.3 47.5 %copy-start.9 = (s32[2]{0:T(128)S(1)}, s32[2]{0:T(128)}, u32[]{:S(2)}) copy-start(s32[2]{0:T(128)} %param.18) | copy-start | bytes 28
  243.7 4.0 %copy-start.2 = (bf16[1024,4,128]{2,1,0:T(4,128)(2,1)S(1)}, bf16[1024,4,128]{2,1,0:T(4,128)(2,1)}, u32[]{:S(2)}) copy-start(bf16[1024,4,128]{2,1,0:T(4,128)(2,1)} %squeeze.30) | copy-start | bytes 3145732 | tf_op jit(solution)/shard_map/while
  267.9 4.0 %copy-start.2 = (bf16[1024,4,128]{2,1,0:T(4,128)(2,1)S(1)}, bf16[1024,4,128]{2,1,0:T(4,128)(2,1)}, u32[]{:S(2)}) copy-start(bf16[1024,4,128]{2,1,0:T(4,128)(2,1)} %squeeze.30) | copy-start | bytes 3145732 | tf_op jit(solution)/shard_map/while
  278.3 0.7 copy-start.1
Sparse Core Ops, SparseCore 0:
  9.0 203.3 all-gather.1
where the time goes:
time: 287 us; the launch traced here: 286 us
  waiting for transfers between devices  148 us (52%)
  local copies, waits for them, and re-layouts  37.2 us (13%)
  other arithmetic  31.4 us (11%)
  matrix products  31.2 us (11%)
  between operations  23.2 us (8%)
  starting transfers between devices  12.4 us (4%)
    ppermute x8, waiting for transfers between devices, passed_along(): return lax.ppermute(block, axis, route)  117 us
    all_gather x1, waiting for transfers between devices, shards(): whole_weight = lax.all_gather(q_weight, 'blk', axis=0, tiled=True)  30 us
    dot_general x1, matrix products, shards(): jnp.dot(normed, whole_weight, preferred_element_type=jnp.float32)  17.5 us
    ppermute x8, starting transfers between devices, passed_along(): return lax.ppermute(block, axis, route)  12.3 us
    reduce_sum x2, other arithmetic, attend_single(): denominator = jnp.sum(exponent, axis=-1)  7.9 us
    dot_general x2, matrix products, attend_single(): jnp.einsum('rkgt,tkd->rkgd', weights, block_value_rows, preferred_element...  7.83 us
    select_n x2, other arithmetic, select_block(): return jnp.where(has_block, chosen, empty_block)  6.33 us
    dynamic_slice x8, local copies, waits for them, and re-layouts, attend_all(): lax.map(attend_single, (shaped, sketch_blocks, block_lists, hole_starts,...  6.01 us
  transfers between devices with their start and end apart: 9, of which 5 were waited for; matrix products, arithmetic and copies ran while one was open for 12% of the time, Pallas kernels for 0%

commit v1 on v0

--- a/solution.py
+++ b/solution.py
@@ -65,7 +65,12 @@
 
 def shards(hidden, norm_gain, q_weight, q_bias, kv_store, block_home, need_ids, hole_pos, fill_len):
     normed = rms_normed(hidden, norm_gain)
-    whole_weight = lax.all_gather(q_weight, "blk", axis=0, tiled=True)
+    ring = [q_weight]
+    for hop in range(15):
+        ring.append(lax.ppermute(ring[-1], "blk", [(dev, (dev + 1) % 16) for dev in range(16)]))
+    whole_weight = jnp.roll(
+        jnp.concatenate(ring[::-1], axis=0), (lax.axis_index("blk") + 1) * ring[0].shape[0], axis=0
+    )
     projected = jnp.dot(normed, whole_weight, preferred_element_type=jnp.float32)
     query = (projected + q_bias).astype(jnp.bfloat16)
     device_count = lax.axis_size("blk")

time: 287 us -> 559 us (1.95)
  waiting for transfers between devices: 148 us -> 312 us
  local copies, waits for them, and re-layouts: 37.2 us -> 108 us
  starting transfers between devices: 12.4 us -> 46.4 us
  between operations: 23.2 us -> 9.84 us
  matrix products: 31.2 us -> 39.6 us
    ppermute x0 -> x15, waiting for transfers between devices: none -> 282 us  [shards(): lax.ppermute(ring[-1], 'blk', [(dev, (dev + 1) % 16) for dev in range(16)])]
    ppermute x8, waiting for transfers between devices: 117 us -> 30.2 us  [passed_along(): return lax.ppermute(block, axis, route)]
    unnamed x21 -> x82, local copies, waits for them, and re-layouts: 4.33 us -> 72.1 us
    all_gather x1 -> x0, waiting for transfers between devices: 30 us -> none  [shards(): whole_weight = lax.all_gather(q_weight, 'blk', axis=0, tiled=True)]
    ppermute x0 -> x15, starting transfers between devices: none -> 26.8 us  [shards(): lax.ppermute(ring[-1], 'blk', [(dev, (dev + 1) % 16) for dev in range(16)])]
    ppermute x8, starting transfers between devices: 12.3 us -> 19.6 us  [passed_along(): return lax.ppermute(block, axis, route)]
    dot_general x2, matrix products: 7.83 us -> 15 us  [attend_single(): jnp.einsum('rkgt,tkd->rkgd', weights, block_value_rows, preferred_element...]
  transfers between devices with their start and end apart: 9 -> 23, of which waited for: 5 -> 17; matrix products, arithmetic and copies ran while one was open for 12% -> 8% of each run, Pallas kernels for 0% -> 0%
where the time goes in v1:
time: 559 us; the launch traced here: 555 us
  waiting for transfers between devices  312 us (56%)
  local copies, waits for them, and re-layouts  108 us (19%)
  starting transfers between devices  46.4 us (8%)
  matrix products  39.6 us (7%)
  other arithmetic  35.6 us (6%)
  between operations  9.84 us (2%)
    ppermute x15, waiting for transfers between devices, shards(): lax.ppermute(ring[-1], 'blk', [(dev, (dev + 1) % 16) for dev in range(16)])  282 us
    unnamed x82, local copies, waits for them, and re-layouts  72.1 us
    ppermute x8, waiting for transfers between devices, passed_along(): return lax.ppermute(block, axis, route)  30.2 us
    ppermute x15, starting transfers between devices, shards(): lax.ppermute(ring[-1], 'blk', [(dev, (dev + 1) % 16) for dev in range(16)])  26.8 us
    ppermute x8, starting transfers between devices, passed_along(): return lax.ppermute(block, axis, route)  19.6 us
    dot_general x1, matrix products, shards(): jnp.dot(normed, whole_weight, preferred_element_type=jnp.float32)  18.7 us
    dot_general x2, matrix products, attend_single(): jnp.einsum('rkgt,tkd->rkgd', weights, block_value_rows, preferred_element...  15 us
  transfers between devices with their start and end apart: 23, of which 17 were waited for; matrix products, arithmetic and copies ran while one was open for 8% of the time, Pallas kernels for 0%

profile of v1, /device:TPU:0, one launch (start us, length us, event | category | flops | bytes accessed | tf_op | source)
XLA Modules:
  0.0 554.7 jit_solution(5721299861481210060)
XLA Ops:
  0.5 24.0 %collective-permute-done.8 = bf16[320,2560]{1,0:T(8,128)(2,1)S(1)} collective-permute-done((bf16[320,2560]{1,0:T(8,128)(2,1)}, bf16[320,2560]{1,0:T(8,128)(2,1)S(1)}, u32[]{:S(2)}, u32[]{:S(2)}) %collective-permute-start.8) | collective-permute-done | bytes 1638432 | tf_op jit(solution)/shard_map/ppermute | solution.py:70
  24.5 23.2 %collective-permute-done.9 = bf16[320,2560]{1,0:T(8,128)(2,1)S(1)} collective-permute-done((bf16[320,2560]{1,0:T(8,128)(2,1)S(1)}, bf16[320,2560]{1,0:T(8,128)(2,1)S(1)}, u32[]{:S(2)}, u32[]{:S(2)}) %collective-permute-start.9) | collective-permute-done | bytes 1638432 | tf_op jit(solution)/shard_map/ppermute | solution.py:70
  47.7 23.2 %collective-permute-done.10 = bf16[320,2560]{1,0:T(8,128)(2,1)S(1)} collective-permute-done((bf16[320,2560]{1,0:T(8,128)(2,1)S(1)}, bf16[320,2560]{1,0:T(8,128)(2,1)S(1)}, u32[]{:S(2)}, u32[]{:S(2)}) %collective-permute-start.10) | collective-permute-done | bytes 1638432 | tf_op jit(solution)/shard_map/ppermute | solution.py:70
  72.1 23.2 %collective-permute-done.11 = bf16[320,2560]{1,0:T(8,128)(2,1)S(1)} collective-permute-done((bf16[320,2560]{1,0:T(8,128)(2,1)S(1)}, bf16[320,2560]{1,0:T(8,128)(2,1)S(1)}, u32[]{:S(2)}, u32[]{:S(2)}) %collective-permute-start.11) | collective-permute-done | bytes 1638432 | tf_op jit(solution)/shard_map/ppermute | solution.py:70
  96.6 23.2 %collective-permute-done.12 = bf16[320,2560]{1,0:T(8,128)(2,1)S(1)} collective-permute-done((bf16[320,2560]{1,0:T(8,128)(2,1)S(1)}, bf16[320,2560]{1,0:T(8,128)(2,1)S(1)}, u32[]{:S(2)}, u32[]{:S(2)}) %collective-permute-start.12) | collective-permute-done | bytes 1638432 | tf_op jit(solution)/shard_map/ppermute | solution.py:70
  121.0 23.2 %collective-permute-done.13 = bf16[320,2560]{1,0:T(8,128)(2,1)S(1)} collective-permute-done((bf16[320,2560]{1,0:T(8,128)(2,1)S(1)}, bf16[320,2560]{1,0:T(8,128)(2,1)S(1)}, u32[]{:S(2)}, u32[]{:S(2)}) %collective-permute-start.13) | collective-permute-done | bytes 1638432 | tf_op jit(solution)/shard_map/ppermute | solution.py:70
  145.4 23.2 %collective-permute-done.14 = bf16[320,2560]{1,0:T(8,128)(2,1)S(1)} collective-permute-done((bf16[320,2560]{1,0:T(8,128)(2,1)S(1)}, bf16[320,2560]{1,0:T(8,128)(2,1)S(1)}, u32[]{:S(2)}, u32[]{:S(2)}) %collective-permute-start.14) | collective-permute-done | bytes 1638432 | tf_op jit(solution)/shard_map/ppermute | solution.py:70
  169.8 23.2 %collective-permute-done.15 = bf16[320,2560]{1,0:T(8,128)(2,1)S(1)} collective-permute-done((bf16[320,2560]{1,0:T(8,128)(2,1)S(1)}, bf16[320,2560]{1,0:T(8,128)(2,1)S(1)}, u32[]{:S(2)}, u32[]{:S(2)}) %collective-permute-start.15) | collective-permute-done | bytes 1638432 | tf_op jit(solution)/shard_map/ppermute | solution.py:70
  194.3 23.2 %collective-permute-done.16 = bf16[320,2560]{1,0:T(8,128)(2,1)S(1)} collective-permute-done((bf16[320,2560]{1,0:T(8,128)(2,1)S(1)}, bf16[320,2560]{1,0:T(8,128)(2,1)S(1)}, u32[]{:S(2)}, u32[]{:S(2)}) %collective-permute-start.16) | collective-permute-done | bytes 1638432 | tf_op jit(solution)/shard_map/ppermute | solution.py:70
  218.7 23.2 %collective-permute-done.17 = bf16[320,2560]{1,0:T(8,128)(2,1)S(1)} collective-permute-done((bf16[320,2560]{1,0:T(8,128)(2,1)S(1)}, bf16[320,2560]{1,0:T(8,128)(2,1)S(1)}, u32[]{:S(2)}, u32[]{:S(2)}) %collective-permute-start.17) | collective-permute-done | bytes 1638432 | tf_op jit(solution)/shard_map/ppermute | solution.py:70
  243.2 23.4 %collective-permute-done.18 = bf16[320,2560]{1,0:T(8,128)(2,1)} collective-permute-done((bf16[320,2560]{1,0:T(8,128)(2,1)S(1)}, bf16[320,2560]{1,0:T(8,128)(2,1)}, u32[]{:S(2)}, u32[]{:S(2)}) %collective-permute-start.18) | collective-permute-done | bytes 1638432 | tf_op jit(solution)/shard_map/ppermute | solution.py:70
  266.5 4.5 collective-permute-start.4
  279.4 10.7 %collective-permute-done.19 = bf16[320,2560]{1,0:T(8,128)(2,1)} collective-permute-done((bf16[320,2560]{1,0:T(8,128)(2,1)}, bf16[320,2560]{1,0:T(8,128)(2,1)}, u32[]{:S(2)}, u32[]{:S(2)}) %collective-permute-start.19) | collective-permute-done | bytes 1638432 | tf_op jit(solution)/shard_map/ppermute | solution.py:70
  297.6 4.3 select_bitcast_fusion.2
  301.9 4.3 collective-permute-start.3
  306.4 7.4 %collective-permute-done.20 = bf16[320,2560]{1,0:T(8,128)(2,1)} collective-permute-done((bf16[320,2560]{1,0:T(8,128)(2,1)}, bf16[320,2560]{1,0:T(8,128)(2,1)}, u32[]{:S(2)}, u32[]{:S(2)}) %collective-permute-start.20) | collective-permute-done | bytes 1638432 | tf_op jit(solution)/shard_map/ppermute | solution.py:70
  313.8 25.9 %collective-permute-start.21 = (bf16[320,2560]{1,0:T(8,128)(2,1)}, bf16[320,2560]{1,0:T(8,128)(2,1)}, u32[]{:S(2)}, u32[]{:S(2)}) collective-permute-start(bf16[320,2560]{1,0:T(8,128)(2,1)} %collective-permute-done.20), channel_id=1, source_target_pairs={{0,1},{1,2},{2,3},{3,4},{4,5},{5,6},{6,7},{7,8},{8,9},{9,10},{10,1... | collective-permute-start | bytes 4915208 | tf_op jit(solution)/shard_map/ppermute | solution.py:70
  347.0 6.7 %collective-permute-done.1 = bf16[2,512,512]{2,1,0:T(8,128)(2,1)} collective-permute-done((bf16[2,512,512]{2,1,0:T(8,128)(2,1)}, bf16[2,512,512]{2,1,0:T(8,128)(2,1)}, u32[]{:S(2)}, u32[]{:S(2)}) %collective-permute-start.1) | collective-permute-done | bytes 1048608 | tf_op jit(solution)/shard_map/ppermute | solution.py:18
  358.3 5.8 %select_bitcast_fusion = (bf16[2,512,512]{2,1,0:T(8,128)(2,1)}, bf16[5,2,512,512]{3,2,1,0:T(8,128)(2,1)}, bf16[2,512,512]{2,1,0:T(8,128)(2,1)}) fusion(bf16[4,2,512,512]{3,2,1,0:T(8,128)(2,1)} %param.15, s32[]{:T(128)S(6)} %select_n.292, pred[]{:T(512)} %get-tuple-element.71, bf16[5,2,512,512]{3,2,1,0:T(8,128)(2,1)} %bitcast_dynamic-update-slice_fusion.2, ...), kind=kLoop, calls=%fused_computation.47 | loop fusion | flops 1572864 | bytes 6293004 | tf_op jit(solution)/shard_map/jit(_where)/select_n | solution.py:87
  364.1 8.8 %collective-permute-start.5 = (bf16[2,512,512]{2,1,0:T(8,128)(2,1)}, bf16[2,512,512]{2,1,0:T(8,128)(2,1)}, u32[]{:S(2)}, u32[]{:S(2)}) collective-permute-start(bf16[2,512,512]{2,1,0:T(8,128)(2,1)} %get-tuple-element.87), channel_id=1, source_target_pairs={{15,0},{0,1},{1,2},{2,3},{3,4},{4,5},{5,6},{6,7},{7,8},{8,9},{9,10... | collective-permute-start | bytes 3145736 | tf_op jit(solution)/shard_map/ppermute | solution.py:18
  373.3 3.0 fusion.17
  376.3 6.8 %collective-permute-done.5 = bf16[2,512,512]{2,1,0:T(8,128)(2,1)} collective-permute-done((bf16[2,512,512]{2,1,0:T(8,128)(2,1)}, bf16[2,512,512]{2,1,0:T(8,128)(2,1)}, u32[]{:S(2)}, u32[]{:S(2)}) %collective-permute-start.5) | collective-permute-done | bytes 1048608 | tf_op jit(solution)/shard_map/ppermute | solution.py:18
  385.3 16.7 %collective-permute-done.7 = bf16[2,512,512]{2,1,0:T(8,128)(2,1)} collective-permute-done((bf16[2,512,512]{2,1,0:T(8,128)(2,1)}, bf16[2,512,512]{2,1,0:T(8,128)(2,1)}, u32[]{:S(2)}, u32[]{:S(2)}) %collective-permute-start.7) | collective-permute-done | bytes 1048608 | tf_op jit(solution)/shard_map/ppermute | solution.py:18
  404.3 5.3 gather_fusion.6
  409.6 4.6 broadcast_select_fusion
  414.2 7.1 %collective-permute-done.22 = bf16[320,2560]{1,0:T(8,128)(2,1)} collective-permute-done((bf16[320,2560]{1,0:T(8,128)(2,1)}, bf16[320,2560]{1,0:T(8,128)(2,1)}, u32[]{:S(2)}, u32[]{:S(2)}) %collective-permute-start.22) | collective-permute-done | bytes 1638432 | tf_op jit(solution)/shard_map/ppermute | solution.py:70
  477.7 18.7 %fusion.23 = bf16[384,2560]{1,0:T(8,128)(2,1)} fusion(bf16[10240,2560]{1,0:T(8,128)(2,1)} %constant_dynamic-update-slice_fusion.1, s32[]{:T(128)S(6)} %select_n.300, bf16[384,5120]{1,0:T(8,128)(2,1)} %param.11, f32[5120]{0:T(1024)S(1)} %copy-done.21, f32[384]{0:T(512)S(1)} %add_rsqrt_fusion, f32[2560]{0:T(1024)S(1)} %copy-done.22), kind=kOutput, calls=%fused_computation.39 | convolution fusion | flops 10076160000 | bytes 32144900 | tf_op jit(solution)/shard_map/dot_general | solution.py:74
  496.4 57.7 %while.10 = (s32[]{:T(128)}, bf16[2,192,2560]{2,1,0:T(8,128)(2,1)}, s32[2]{0:T(128)S(1)}, bf16[2,2,2,512,512]{4,3,2,1,0:T(8,128)(2,1)}, s32[2,2]{1,0:T(2,128)S(1...) while((s32[]{:T(128)}, bf16[2,192,2560]{2,1,0:T(8,128)(2,1)}, s32[2]{0:T(128)S(1)}, ...), condition=%wide.region_14.15_spmd, body=%wide.region_11.14_spmd.sunk | while | flops 2057990912 | bytes 138627664 | solution.py:62
  508.9 4.1 fusion.55
  514.7 7.5 %bitcast_divide_fusion.2 = bf16[192,4,5,128]{3,0,2,1:T(8,128)(2,1)S(1)} fusion(f32[4,1024,192,5]{1,2,3,0:T(8,128)} %copy-done.2, f32[192,4,5]{0,2,1:T(8,128)S(1)} %get-tuple-element.145, pred[1024]{0:T(1024)(128)(4,1)S(1)} %and.185, bf16[1024,4,128,1]{2,1,0,3:T(4,128)(2,1)S(1)} %bitcast.93, f32[192,4,5]{0,2,1:T(8,128)S(1)} %fusion.55), kind=kOutput, calls=%fused_computation.17.clone.1 | convolution fusion | flops 1023344640 | bytes 17792000 | tf_op jit(solution)/shard_map/while/body/eval_jaxpr/rkgt,tkd->rkgd/dot_general | solution.py:50
  537.6 4.1 fusion.55
  543.4 7.5 %bitcast_divide_fusion.2 = bf16[192,4,5,128]{3,0,2,1:T(8,128)(2,1)S(1)} fusion(f32[4,1024,192,5]{1,2,3,0:T(8,128)} %copy-done.2, f32[192,4,5]{0,2,1:T(8,128)S(1)} %get-tuple-element.145, pred[1024]{0:T(1024)(128)(4,1)S(1)} %and.185, bf16[1024,4,128,1]{2,1,0,3:T(4,128)(2,1)S(1)} %bitcast.93, f32[192,4,5]{0,2,1:T(8,128)S(1)} %fusion.55), kind=kOutput, calls=%fused_computation.17.clone.1 | convolution fusion | flops 1023344640 | bytes 17792000 | tf_op jit(solution)/shard_map/while/body/eval_jaxpr/rkgt,tkd->rkgd/dot_general | solution.py:50
  (186 shorter events, 121.6 us)
Async XLA Ops:
  0.0 274.6 %copy-start = (s32[64]{0:T(128)S(1)}, s32[64]{0:T(128)}, u32[]{:S(2)}) copy-start(s32[64]{0:T(128)} %param.16) | copy-start | bytes 772
  0.0 24.5 %collective-permute-start.8 = (bf16[320,2560]{1,0:T(8,128)(2,1)}, bf16[320,2560]{1,0:T(8,128)(2,1)S(1)}, u32[]{:S(2)}, u32[]{:S(2)}) collective-permute-start(bf16[320,2560]{1,0:T(8,128)(2,1)} %param.13), channel_id=1, source_target_pairs={{0,1},{1,2},{2,3},{3,4},{4,5},{5,6},{6,7},{7,8},{8,9},{9,10},{10,1... | collective-permute-start | bytes 4915208 | tf_op jit(solution)/shard_map/ppermute | solution.py:70
  24.5 23.2 %collective-permute-start.9 = (bf16[320,2560]{1,0:T(8,128)(2,1)S(1)}, bf16[320,2560]{1,0:T(8,128)(2,1)S(1)}, u32[]{:S(2)}, u32[]{:S(2)}) collective-permute-start(bf16[320,2560]{1,0:T(8,128)(2,1)S(1)} %collective-permute-done.8), channel_id=1, source_target_pairs={{0,1},{1,2},{2,3},{3,4},{4,5},{5,6},{6,7},{7,8},{8,9},{9,10},{10,1... | collective-permute-start | bytes 4915208 | tf_op jit(solution)/shard_map/ppermute | solution.py:70
  47.7 23.2 %collective-permute-start.10 = (bf16[320,2560]{1,0:T(8,128)(2,1)S(1)}, bf16[320,2560]{1,0:T(8,128)(2,1)S(1)}, u32[]{:S(2)}, u32[]{:S(2)}) collective-permute-start(bf16[320,2560]{1,0:T(8,128)(2,1)S(1)} %collective-permute-done.9), channel_id=1, source_target_pairs={{0,1},{1,2},{2,3},{3,4},{4,5},{5,6},{6,7},{7,8},{8,9},{9,10},{10,1... | collective-permute-start | bytes 4915208 | tf_op jit(solution)/shard_map/ppermute | solution.py:70
  72.1 23.2 %collective-permute-start.11 = (bf16[320,2560]{1,0:T(8,128)(2,1)S(1)}, bf16[320,2560]{1,0:T(8,128)(2,1)S(1)}, u32[]{:S(2)}, u32[]{:S(2)}) collective-permute-start(bf16[320,2560]{1,0:T(8,128)(2,1)S(1)} %collective-permute-done.10), channel_id=1, source_target_pairs={{0,1},{1,2},{2,3},{3,4},{4,5},{5,6},{6,7},{7,8},{8,9},{9,10},{10,1... | collective-permute-start | bytes 4915208 | tf_op jit(solution)/shard_map/ppermute | solution.py:70
  96.5 23.2 %collective-permute-start.12 = (bf16[320,2560]{1,0:T(8,128)(2,1)S(1)}, bf16[320,2560]{1,0:T(8,128)(2,1)S(1)}, u32[]{:S(2)}, u32[]{:S(2)}) collective-permute-start(bf16[320,2560]{1,0:T(8,128)(2,1)S(1)} %collective-permute-done.11), channel_id=1, source_target_pairs={{0,1},{1,2},{2,3},{3,4},{4,5},{5,6},{6,7},{7,8},{8,9},{9,10},{10,1... | collective-permute-start | bytes 4915208 | tf_op jit(solution)/shard_map/ppermute | solution.py:70
  121.0 23.2 %collective-permute-start.13 = (bf16[320,2560]{1,0:T(8,128)(2,1)S(1)}, bf16[320,2560]{1,0:T(8,128)(2,1)S(1)}, u32[]{:S(2)}, u32[]{:S(2)}) collective-permute-start(bf16[320,2560]{1,0:T(8,128)(2,1)S(1)} %collective-permute-done.12), channel_id=1, source_target_pairs={{0,1},{1,2},{2,3},{3,4},{4,5},{5,6},{6,7},{7,8},{8,9},{9,10},{10,1... | collective-permute-start | bytes 4915208 | tf_op jit(solution)/shard_map/ppermute | solution.py:70
  145.4 23.2 %collective-permute-start.14 = (bf16[320,2560]{1,0:T(8,128)(2,1)S(1)}, bf16[320,2560]{1,0:T(8,128)(2,1)S(1)}, u32[]{:S(2)}, u32[]{:S(2)}) collective-permute-start(bf16[320,2560]{1,0:T(8,128)(2,1)S(1)} %collective-permute-done.13), channel_id=1, source_target_pairs={{0,1},{1,2},{2,3},{3,4},{4,5},{5,6},{6,7},{7,8},{8,9},{9,10},{10,1... | collective-permute-start | bytes 4915208 | tf_op jit(solution)/shard_map/ppermute | solution.py:70
  169.8 23.2 %collective-permute-start.15 = (bf16[320,2560]{1,0:T(8,128)(2,1)S(1)}, bf16[320,2560]{1,0:T(8,128)(2,1)S(1)}, u32[]{:S(2)}, u32[]{:S(2)}) collective-permute-start(bf16[320,2560]{1,0:T(8,128)(2,1)S(1)} %collective-permute-done.14), channel_id=1, source_target_pairs={{0,1},{1,2},{2,3},{3,4},{4,5},{5,6},{6,7},{7,8},{8,9},{9,10},{10,1... | collective-permute-start | bytes 4915208 | tf_op jit(solution)/shard_map/ppermute | solution.py:70
  194.3 23.2 %collective-permute-start.16 = (bf16[320,2560]{1,0:T(8,128)(2,1)S(1)}, bf16[320,2560]{1,0:T(8,128)(2,1)S(1)}, u32[]{:S(2)}, u32[]{:S(2)}) collective-permute-start(bf16[320,2560]{1,0:T(8,128)(2,1)S(1)} %collective-permute-done.15), channel_id=1, source_target_pairs={{0,1},{1,2},{2,3},{3,4},{4,5},{5,6},{6,7},{7,8},{8,9},{9,10},{10,1... | collective-permute-start | bytes 4915208 | tf_op jit(solution)/shard_map/ppermute | solution.py:70
  218.7 23.2 %collective-permute-start.17 = (bf16[320,2560]{1,0:T(8,128)(2,1)S(1)}, bf16[320,2560]{1,0:T(8,128)(2,1)S(1)}, u32[]{:S(2)}, u32[]{:S(2)}) collective-permute-start(bf16[320,2560]{1,0:T(8,128)(2,1)S(1)} %collective-permute-done.16), channel_id=1, source_target_pairs={{0,1},{1,2},{2,3},{3,4},{4,5},{5,6},{6,7},{7,8},{8,9},{9,10},{10,1... | collective-permute-start | bytes 4915208 | tf_op jit(solution)/shard_map/ppermute | solution.py:70
  243.2 23.4 %collective-permute-start.18 = (bf16[320,2560]{1,0:T(8,128)(2,1)S(1)}, bf16[320,2560]{1,0:T(8,128)(2,1)}, u32[]{:S(2)}, u32[]{:S(2)}) collective-permute-start(bf16[320,2560]{1,0:T(8,128)(2,1)S(1)} %collective-permute-done.17), channel_id=1, source_target_pairs={{0,1},{1,2},{2,3},{3,4},{4,5},{5,6},{6,7},{7,8},{8,9},{9,10},{10,1... | collective-permute-start | bytes 4915208 | tf_op jit(solution)/shard_map/ppermute | solution.py:70
  266.5 23.6 %collective-permute-start.19 = (bf16[320,2560]{1,0:T(8,128)(2,1)}, bf16[320,2560]{1,0:T(8,128)(2,1)}, u32[]{:S(2)}, u32[]{:S(2)}) collective-permute-start(bf16[320,2560]{1,0:T(8,128)(2,1)} %collective-permute-done.18), channel_id=1, source_target_pairs={{0,1},{1,2},{2,3},{3,4},{4,5},{5,6},{6,7},{7,8},{8,9},{9,10},{10,1... | collective-permute-start | bytes 4915208 | tf_op jit(solution)/shard_map/ppermute | solution.py:70
  266.5 12.8 %collective-permute-start = (s32[2,2]{1,0:T(2,128)}, s32[2,2]{1,0:T(2,128)S(1)}, u32[]{:S(2)}, u32[]{:S(2)}) collective-permute-start(s32[2,2]{1,0:T(2,128)} %param.17), channel_id=1, source_target_pairs={{14,0},{15,1},{0,2},{1,3},{2,4},{3,5},{4,6},{5,7},{6,8},{7,9},{8,1... | collective-permute-start | bytes 56 | tf_op jit(solution)/shard_map/ppermute | solution.py:18
  266.5 24.4 %collective-permute-start.2 = (s32[2,2]{1,0:T(2,128)}, s32[2,2]{1,0:T(2,128)S(1)}, u32[]{:S(2)}, u32[]{:S(2)}) collective-permute-start(s32[2,2]{1,0:T(2,128)} %param.17), channel_id=1, source_target_pairs={{15,0},{0,1},{1,2},{2,3},{3,4},{4,5},{5,6},{6,7},{7,8},{8,9},{9,10... | collective-permute-start | bytes 56 | tf_op jit(solution)/shard_map/ppermute | solution.py:18
  266.5 39.6 %collective-permute-start.4 = (s32[2,2]{1,0:T(2,128)}, s32[2,2]{1,0:T(2,128)S(1)}, u32[]{:S(2)}, u32[]{:S(2)}) collective-permute-start(s32[2,2]{1,0:T(2,128)} %param.17), channel_id=1, source_target_pairs={{1,0},{2,1},{3,2},{4,3},{5,4},{6,5},{7,6},{8,7},{9,8},{10,9},{11,1... | collective-permute-start | bytes 56 | tf_op jit(solution)/shard_map/ppermute | solution.py:18
  271.0 35.2 %collective-permute-start.6 = (s32[2,2]{1,0:T(2,128)}, s32[2,2]{1,0:T(2,128)S(1)}, u32[]{:S(2)}, u32[]{:S(2)}) collective-permute-start(s32[2,2]{1,0:T(2,128)} %param.17), channel_id=1, source_target_pairs={{2,0},{3,1},{4,2},{5,3},{6,4},{7,5},{8,6},{9,7},{10,8},{11,9},{12,... | collective-permute-start | bytes 56 | tf_op jit(solution)/shard_map/ppermute | solution.py:18
  290.1 23.7 %collective-permute-start.20 = (bf16[320,2560]{1,0:T(8,128)(2,1)}, bf16[320,2560]{1,0:T(8,128)(2,1)}, u32[]{:S(2)}, u32[]{:S(2)}) collective-permute-start(bf16[320,2560]{1,0:T(8,128)(2,1)} %collective-permute-done.19), channel_id=1, source_target_pairs={{0,1},{1,2},{2,3},{3,4},{4,5},{5,6},{6,7},{7,8},{8,9},{9,10},{10,1... | collective-permute-start | bytes 4915208 | tf_op jit(solution)/shard_map/ppermute | solution.py:70
  301.9 51.8 %collective-permute-start.1 = (bf16[2,512,512]{2,1,0:T(8,128)(2,1)}, bf16[2,512,512]{2,1,0:T(8,128)(2,1)}, u32[]{:S(2)}, u32[]{:S(2)}) collective-permute-start(bf16[2,512,512]{2,1,0:T(8,128)(2,1)} %get-tuple-element.89), channel_id=1, source_target_pairs={{2,0},{3,1},{4,2},{5,3},{6,4},{7,5},{8,6},{9,7},{10,8},{11,9},{12,... | collective-permute-start | bytes 3145736 | tf_op jit(solution)/shard_map/ppermute | solution.py:18
  301.9 54.1 %collective-permute-start.3 = (bf16[2,512,512]{2,1,0:T(8,128)(2,1)}, bf16[2,512,512]{2,1,0:T(8,128)(2,1)}, u32[]{:S(2)}, u32[]{:S(2)}) collective-permute-start(bf16[2,512,512]{2,1,0:T(8,128)(2,1)} %get-tuple-element.88), channel_id=1, source_target_pairs={{1,0},{2,1},{3,2},{4,3},{5,4},{6,5},{7,6},{8,7},{9,8},{10,9},{11,1... | collective-permute-start | bytes 3145736 | tf_op jit(solution)/shard_map/ppermute | solution.py:18
  313.8 59.3 %collective-permute-start.21 = (bf16[320,2560]{1,0:T(8,128)(2,1)}, bf16[320,2560]{1,0:T(8,128)(2,1)}, u32[]{:S(2)}, u32[]{:S(2)}) collective-permute-start(bf16[320,2560]{1,0:T(8,128)(2,1)} %collective-permute-done.20), channel_id=1, source_target_pairs={{0,1},{1,2},{2,3},{3,4},{4,5},{5,6},{6,7},{7,8},{8,9},{9,10},{10,1... | collective-permute-start | bytes 4915208 | tf_op jit(solution)/shard_map/ppermute | solution.py:70
  364.1 19.0 %collective-permute-start.5 = (bf16[2,512,512]{2,1,0:T(8,128)(2,1)}, bf16[2,512,512]{2,1,0:T(8,128)(2,1)}, u32[]{:S(2)}, u32[]{:S(2)}) collective-permute-start(bf16[2,512,512]{2,1,0:T(8,128)(2,1)} %get-tuple-element.87), channel_id=1, source_target_pairs={{15,0},{0,1},{1,2},{2,3},{3,4},{4,5},{5,6},{6,7},{7,8},{8,9},{9,10... | collective-permute-start | bytes 3145736 | tf_op jit(solution)/shard_map/ppermute | solution.py:18
  372.9 29.2 %collective-permute-start.7 = (bf16[2,512,512]{2,1,0:T(8,128)(2,1)}, bf16[2,512,512]{2,1,0:T(8,128)(2,1)}, u32[]{:S(2)}, u32[]{:S(2)}) collective-permute-start(bf16[2,512,512]{2,1,0:T(8,128)(2,1)} %get-tuple-element.85), channel_id=1, source_target_pairs={{14,0},{15,1},{0,2},{1,3},{2,4},{3,5},{4,6},{5,7},{6,8},{7,9},{8,1... | collective-permute-start | bytes 3145736 | tf_op jit(solution)/shard_map/ppermute | solution.py:18
  373.1 48.2 %collective-permute-start.22 = (bf16[320,2560]{1,0:T(8,128)(2,1)}, bf16[320,2560]{1,0:T(8,128)(2,1)}, u32[]{:S(2)}, u32[]{:S(2)}) collective-permute-start(bf16[320,2560]{1,0:T(8,128)(2,1)} %collective-permute-done.21), channel_id=1, source_target_pairs={{0,1},{1,2},{2,3},{3,4},{4,5},{5,6},{6,7},{7,8},{8,9},{9,10},{10,1... | collective-permute-start | bytes 4915208 | tf_op jit(solution)/shard_map/ppermute | solution.py:70
  414.2 21.3 %copy-start.19 = (bf16[320,2560]{1,0:T(8,128)(2,1)S(1)}, bf16[320,2560]{1,0:T(8,128)(2,1)}, u32[]{:S(2)}) copy-start(bf16[320,2560]{1,0:T(8,128)(2,1)} %copy-done.18) | copy-start | bytes 4915204
  424.0 12.8 %copy-start.17 = (bf16[320,2560]{1,0:T(8,128)(2,1)S(1)}, bf16[320,2560]{1,0:T(8,128)(2,1)}, u32[]{:S(2)}) copy-start(bf16[320,2560]{1,0:T(8,128)(2,1)} %copy-done.16) | copy-start | bytes 4915204
  426.9 11.2 %copy-start.15 = (bf16[320,2560]{1,0:T(8,128)(2,1)S(1)}, bf16[320,2560]{1,0:T(8,128)(2,1)}, u32[]{:S(2)}) copy-start(bf16[320,2560]{1,0:T(8,128)(2,1)} %copy-done.14) | copy-start | bytes 4915204
  429.7 9.7 %copy-start.13 = (bf16[320,2560]{1,0:T(8,128)(2,1)S(1)}, bf16[320,2560]{1,0:T(8,128)(2,1)}, u32[]{:S(2)}) copy-start(bf16[320,2560]{1,0:T(8,128)(2,1)} %copy-done.12) | copy-start | bytes 4915204
  432.6 8.1 %copy-start.11 = (bf16[320,2560]{1,0:T(8,128)(2,1)S(1)}, bf16[320,2560]{1,0:T(8,128)(2,1)}, u32[]{:S(2)}) copy-start(bf16[320,2560]{1,0:T(8,128)(2,1)} %copy-done.10) | copy-start | bytes 4915204
  477.6 18.7 %copy-start.20 = (s32[2,2]{1,0:T(2,128)S(1)}, s32[2,2]{1,0:T(2,128)}, u32[]{:S(2)}) copy-start(s32[2,2]{1,0:T(2,128)} %param.17) | copy-start | bytes 52
  477.6 18.7 %copy-start.23 = (s32[2]{0:T(128)S(1)}, s32[2]{0:T(128)}, u32[]{:S(2)}) copy-start(s32[2]{0:T(128)} %param.19) | copy-start | bytes 28
  477.7 18.7 %copy-start.24 = (s32[2]{0:T(128)S(1)}, s32[2]{0:T(128)}, u32[]{:S(2)}) copy-start(s32[2]{0:T(128)} %param.18) | copy-start | bytes 28
  (17 other events, 60.2 us)
